TPU v7x, 512 devices: a whole 4x8x8 slice. The times are simulated.
512 devices in a mesh: dom: 128 (over y, z, core), row: 4 (over x).
Axes of the slice: x: 4, y: 8, z: 8, core: 2. Of those that a mesh axis runs over, the one named last changes fastest.
Arguments:
- p_blocks: bfloat16 [1536, 12, 128, 128], P(('dom', 'row')), may hold values from -0.5 to 0.5
- p_cols: int32 [1536, 12], P(('dom', 'row')), may hold values from 0 to 1535, as said below
- sel_square: int32 [1536, 4, 12], P(('dom', 'row')), may hold values from -1 to 1, as said below
- sel_cube: int32 [1536, 4, 12], P(('dom', 'row')), may hold values from -1 to 3, as said below
Outputs:
- purified: bfloat16 [1536, 4, 128, 128], P(('dom', 'row'))
Inputs may be any that keep to these rules, and one draw needn't show every extreme that they name: `p_cols`: the 12 entries of a row are distinct clusters held by devices at most 2 positions away from the row's own device in dom-then-row order, cyclically. `sel_square`: -1 marks a term left out; other values name one of the first 2 stored blocks of row p_cols[i, a]. `sel_cube`: -1 marks a term left out; other values name a block of square of row p_cols[i, a].
All inputs are finite; a program needn't handle non-finite values.
Results may differ from a plain program's by a relative error of at most 0.0043.
Values may be sent and summed in bfloat16 or wider, within the bound.
A program may use at most 64 MiB of HBM per device.

v0:
```python
import jax
import jax.numpy as jnp
from jax import lax
from jax.sharding import PartitionSpec as P

MW = 2


def extended(cells, sides, width):
    for axis, dim in sides:
        count = lax.axis_size(axis)
        head = lax.slice_in_dim(cells, 0, width, axis=dim)
        tail = lax.slice_in_dim(cells, cells.shape[dim] - width, cells.shape[dim], axis=dim)
        cells = jnp.concatenate(
            [
                lax.ppermute(tail, axis, [(i, (i + 1) % count) for i in range(count)]),
                cells,
                lax.ppermute(head, axis, [((i + 1) % count, i) for i in range(count)]),
            ],
            axis=dim,
        )
    return cells


def contract(p_blocks, nearby, local_rows, selection):
    per_row = nearby.shape[1]
    flattened = nearby.reshape((-1,) + nearby.shape[2:])
    results = []
    for column in range(selection.shape[1]):
        picked = selection[:, column, :]
        position = local_rows * per_row + jnp.maximum(picked, 0)
        operand = jnp.take(flattened, position, axis=0)
        operand = jnp.where((picked >= 0)[:, :, None, None], operand, jnp.zeros((), operand.dtype))
        results.append(
            jnp.einsum("iaxy,iayz->ixz", p_blocks, operand, preferred_element_type=jnp.float32)
        )
    return jnp.stack(results, 1)


def per_device(p_blocks, p_cols, sel_square, sel_cube):
    row_count = p_blocks.shape[0]
    dom_count = lax.axis_size("dom")
    group_count = lax.axis_size("row")
    clusters = row_count * dom_count * group_count
    window = p_blocks[:, :MW]
    domain_window = lax.all_gather(window, "row", axis=0, tiled=True)
    nearby_window = extended(domain_window, (("dom", 0),), domain_window.shape[0])
    anchor = (lax.axis_index("dom") - 1) * (group_count * row_count)
    local_rows = jnp.mod(p_cols - anchor, clusters)
    square = contract(p_blocks, nearby_window, local_rows, sel_square)
    square_round = square.astype(jnp.bfloat16)
    domain_square = lax.all_gather(square_round, "row", axis=0, tiled=True)
    nearby_square = extended(domain_square, (("dom", 0),), domain_square.shape[0])
    cube = contract(p_blocks, nearby_square, local_rows, sel_cube)
    return (3.0 * square - 2.0 * cube).astype(jnp.bfloat16)


def solution(mesh):
    return jax.shard_map(
        per_device,
        mesh=mesh,
        in_specs=(
            P(("dom", "row"), None, None, None),
            P(("dom", "row"), None),
            P(("dom", "row"), None, None),
            P(("dom", "row"), None, None),
        ),
        out_specs=P(("dom", "row"), None, None, None),
        check_vma=False,
    )
```

profile of v0, /device:TPU:1, one launch (start us, length us, event | category | flops | bytes accessed | tf_op | source)
XLA Modules:
  0.0 158.5 jit_solution(687500145116812891)
XLA Ops:
  6.5 1.0 slice.28
  7.5 11.6 %all_gather.6 = bf16[12,2,128,128]{3,2,1,0:T(8,128)(2,1)S(1)} all-gather(bf16[3,2,128,128]{3,2,1,0:T(8,128)(2,1)S(1)} %slice.28), channel_id=1, replica_groups=mesh['dom'=128,'row'=4] {'row'}, dimensions={0}, use_global_device_ids=true | all-gather | bytes 983040 | tf_op jit(solution)/shard_map/all_gather | solution.py:46
  19.1 7.4 %collective-permute-start = (bf16[12,2,128,128]{3,2,1,0:T(8,128)(2,1)S(1)}, bf16[12,2,128,128]{3,2,1,0:T(8,128)(2,1)S(1)}, u32[]{:S(2)}, u32[]{:S(2)}) collective-permute-start(bf16[12,2,128,128]{3,2,1,0:T(8,128)(2,1)S(1)} %all_gather.6), channel_id=1, source_target_pairs={{0,4},{4,8},{8,12},{12,16},{16,20},{20,24},{24,28},{28,32},{32,36}... | collective-permute-start | bytes 2359304 | tf_op jit(solution)/shard_map/ppermute | solution.py:16
  26.6 5.0 %collective-permute-start.1 = (bf16[12,2,128,128]{3,2,1,0:T(8,128)(2,1)S(1)}, bf16[12,2,128,128]{3,2,1,0:T(8,128)(2,1)}, u32[]{:S(2)}, u32[]{:S(2)}) collective-permute-start(bf16[12,2,128,128]{3,2,1,0:T(8,128)(2,1)S(1)} %all_gather.6), channel_id=1, source_target_pairs={{4,0},{8,4},{12,8},{16,12},{20,16},{24,20},{28,24},{32,28},{36,32}... | collective-permute-start | bytes 2359304 | tf_op jit(solution)/shard_map/ppermute | solution.py:18
  31.6 0.7 compare_and_fusion.3
  32.4 0.1 reshape.174
  32.5 0.1 reshape.178
  32.5 0.6 pad_clamp_fusion.5
  33.1 0.1 reshape.182
  33.2 0.6 pad_clamp_fusion.4
  33.8 0.5 copy_bitcast_fusion.6
  34.4 0.5 copy_bitcast_fusion.4
  34.9 0.6 collective-permute-done
  35.5 0.9 copy-done.4
  36.4 3.8 %collective-permute-done.1 = bf16[12,2,128,128]{3,2,1,0:T(8,128)(2,1)} collective-permute-done((bf16[12,2,128,128]{3,2,1,0:T(8,128)(2,1)S(1)}, bf16[12,2,128,128]{3,2,1,0:T(8,128)(2,1)}, u32[]{:S(2)}, u32[]{:S(2)}) %collective-permute-start.1) | collective-permute-done | bytes 786464 | tf_op jit(solution)/shard_map/ppermute | solution.py:18
  40.2 1.6 %pad_maximum_fusion.1 = bf16[36,2,128,128]{3,2,1,0:T(8,128)(2,1)S(1)} fusion(bf16[12,2,128,128]{3,2,1,0:T(8,128)(2,1)} %collective-permute-done.1, bf16[12,2,128,128]{3,2,1,0:T(8,128)(2,1)S(1)} %all_gather.6, bf16[12,2,128,128]{3,2,1,0:T(8,128)(2,1)} %copy-done.4), kind=kLoop, calls=%fused_computation.9 | loop fusion | flops 2359296 | bytes 4718592 | tf_op jit(solution)/shard_map/concatenate | solution.py:14
  41.8 0.8 gather_fusion
  42.6 1.4 copy.20
  44.0 0.8 gather_fusion.1
  44.8 1.4 copy.21
  46.2 0.8 gather_fusion.2
  47.0 1.4 copy.22
  48.4 0.8 gather_fusion.3
  49.2 0.7 copy.23
  50.0 0.5 copy-done.3
  50.5 1.9 %fusion.24 = f32[3,1,128,128]{2,3,0,1:T(8,128)S(1)} fusion(bf16[3,12,128,128]{3,2,1,0:T(8,128)(2,1)} %param.8, bf16[3,12,128,128]{2,3,1,0:T(8,128)(2,1)S(1)} %bitcast.145, pred[3,12]{1,0:T(4,128)(4,1)S(1)} %copy-done.31, pred[3,12]{1,0:T(4,128)(4,1)S(1)} %copy-done.38), kind=kOutput, calls=%fused_computation.42 | convolution fusion | flops 152174592 | bytes 2555976 | tf_op jit(solution)/shard_map/iaxy,iayz->ixz/dot_general | solution.py:35
  52.5 0.5 fusion.25
  53.1 0.8 copy-done.1
  53.8 0.5 fusion.26
  54.4 0.1 copy-done.28
  54.5 0.5 fusion.27
  55.1 0.7 copy-done.11
  55.7 0.8 fusion.50
  56.6 35.5 %all-gather.2.cloned.1.call-done = bf16[12,4,128,128]{2,3,0,1:T(8,128)(2,1)} async-done(((bf16[3,4,128,128]{2,3,0,1:T(8,128)(2,1)}), bf16[12,4,128,128]{2,3,0,1:T(8,128)(2,1)}) %all-gather.2.cloned.1.call-update) | async-done | bytes 1572880 | tf_op jit(solution)/shard_map/all_gather | solution.py:52
  92.1 3.8 %collective-permute-start.2 = (bf16[12,4,128,128]{2,3,0,1:T(8,128)(2,1)}, bf16[12,4,128,128]{2,3,0,1:T(8,128)(2,1)S(1)}, u32[]{:S(2)}, u32[]{:S(2)}) collective-permute-start(bf16[12,4,128,128]{2,3,0,1:T(8,128)(2,1)} %all-gather.2.cloned.1.call-done), channel_id=1, source_target_pairs={{0,4},{4,8},{8,12},{12,16},{16,20},{20,24},{24,28},{28,32},{32,36}... | collective-permute-start | bytes 4718600 | tf_op jit(solution)/shard_map/ppermute | solution.py:16
  95.9 1.9 %collective-permute-start.3 = (bf16[12,4,128,128]{2,3,0,1:T(8,128)(2,1)}, bf16[12,4,128,128]{2,3,0,1:T(8,128)(2,1)S(1)}, u32[]{:S(2)}, u32[]{:S(2)}) collective-permute-start(bf16[12,4,128,128]{2,3,0,1:T(8,128)(2,1)} %all-gather.2.cloned.1.call-done), channel_id=1, source_target_pairs={{4,0},{8,4},{12,8},{16,12},{20,16},{24,20},{28,24},{32,28},{36,32}... | collective-permute-start | bytes 4718600 | tf_op jit(solution)/shard_map/ppermute | solution.py:18
  97.8 0.1 reshape.186
  97.9 0.1 reshape.190
  98.0 0.1 reshape.194
  98.2 0.5 copy_bitcast_fusion.2
  98.8 0.5 copy_bitcast_fusion
  99.3 14.2 %collective-permute-done.2 = bf16[12,4,128,128]{2,3,0,1:T(8,128)(2,1)S(1)} collective-permute-done((bf16[12,4,128,128]{2,3,0,1:T(8,128)(2,1)}, bf16[12,4,128,128]{2,3,0,1:T(8,128)(2,1)S(1)}, u32[]{:S(2)}, u32[]{:S(2)}) %collective-permute-start.2) | collective-permute-done | bytes 1572896 | tf_op jit(solution)/shard_map/ppermute | solution.py:16
  113.5 4.6 %collective-permute-done.3 = bf16[12,4,128,128]{2,3,0,1:T(8,128)(2,1)S(1)} collective-permute-done((bf16[12,4,128,128]{2,3,0,1:T(8,128)(2,1)}, bf16[12,4,128,128]{2,3,0,1:T(8,128)(2,1)S(1)}, u32[]{:S(2)}, u32[]{:S(2)}) %collective-permute-start.3) | collective-permute-done | bytes 1572896 | tf_op jit(solution)/shard_map/ppermute | solution.py:18
  118.1 3.6 %pad_maximum_fusion = bf16[36,4,128,128]{2,3,0,1:T(8,128)(2,1)} fusion(bf16[12,4,128,128]{2,3,0,1:T(8,128)(2,1)S(1)} %collective-permute-done.3, bf16[12,4,128,128]{2,3,0,1:T(8,128)(2,1)} %all-gather.2.cloned.1.call-done, bf16[12,4,128,128]{2,3,0,1:T(8,128)(2,1)S(1)} %collective-permute-done.2), kind=kLoop, calls=%fused_computation.8 | loop fusion | flops 4718592 | bytes 9437184 | tf_op jit(solution)/shard_map/concatenate | solution.py:14
  121.7 6.6 %copy.24 = bf16[36,4,128,128]{3,2,1,0:T(8,128)(2,1)} copy(bf16[36,4,128,128]{2,3,0,1:T(8,128)(2,1)} %pad_maximum_fusion) | data formatting | bytes 9437184 | tf_op jit(solution)/shard_map/concatenate | solution.py:14
  128.3 3.1 %gather_fusion.4 = bf16[36,128,128]{2,1,0:T(8,128)(2,1)S(1)} fusion(bf16[144,128,128]{2,1,0:T(8,128)(2,1)} %bitcast.134, s32[1024]{0:T(1024)S(1)} %pad_clamp_fusion.3), kind=kCustom, calls=%fused_computation.1.clone | custom fusion | bytes 2359440 | tf_op jit(solution)/shard_map/jit(_take)/gather | solution.py:32
  131.5 1.4 copy.25
  132.9 3.1 %gather_fusion.5 = bf16[36,128,128]{2,1,0:T(8,128)(2,1)S(1)} fusion(bf16[144,128,128]{2,1,0:T(8,128)(2,1)} %bitcast.135, s32[1024]{0:T(1024)S(1)} %pad_clamp_fusion.2), kind=kCustom, calls=%fused_computation.5.clone | custom fusion | bytes 2359440 | tf_op jit(solution)/shard_map/jit(_take)/gather | solution.py:32
  136.0 0.7 copy.26
  136.7 3.1 %gather_fusion.6 = bf16[36,128,128]{2,1,0:T(8,128)(2,1)S(1)} fusion(bf16[144,128,128]{2,1,0:T(8,128)(2,1)} %bitcast.136, s32[1024]{0:T(1024)S(1)} %pad_clamp_fusion.1), kind=kCustom, calls=%fused_computation.6.clone | custom fusion | bytes 2359440 | tf_op jit(solution)/shard_map/jit(_take)/gather | solution.py:32
  139.8 1.4 copy.27
  141.2 3.1 %gather_fusion.7 = bf16[36,128,128]{2,1,0:T(8,128)(2,1)S(1)} fusion(bf16[144,128,128]{2,1,0:T(8,128)(2,1)} %bitcast.137, s32[1024]{0:T(1024)S(1)} %pad_clamp_fusion), kind=kCustom, calls=%fused_computation.7.clone | custom fusion | bytes 2359440 | tf_op jit(solution)/shard_map/jit(_take)/gather | solution.py:32
  144.4 0.7 copy.28
  145.2 2.2 %fusion.28 = f32[3,1,128,128]{2,3,0,1:T(8,128)S(1)} fusion(bf16[3,12,128,128]{3,2,1,0:T(8,128)(2,1)} %param.8, bf16[3,12,128,128]{2,3,1,0:T(8,128)(2,1)} %copy.25, pred[3,12]{1,0:T(4,128)(4,1)S(1)} %copy-done.27, pred[3,12]{1,0:T(4,128)(4,1)S(1)} %copy-done.37), kind=kOutput, calls=%fused_computation.46 | convolution fusion | flops 152174592 | bytes 2555976 | tf_op jit(solution)/shard_map/iaxy,iayz->ixz/dot_general | solution.py:35
  147.5 0.5 fusion.29
  148.0 0.7 copy-done.2
  148.7 0.5 fusion.30
  149.3 0.5 fusion.31
  149.9 0.4 copy-done.6
  150.3 0.1 copy-done.8
  150.3 0.1 copy-done.10
  150.4 0.1 copy-done.12
  150.5 0.1 fusion.33
  150.7 0.9 copy.29
  (81 shorter events, 0.5 us)
Async XLA Ops:
  6.5 25.0 %copy-start.15 = (s32[3,4,12]{2,1,0:T(4,128)S(1)}, s32[3,4,12]{2,1,0:T(4,128)}, u32[]{:S(2)}) copy-start(s32[3,4,12]{2,1,0:T(4,128)} %param.10) | copy-start | bytes 1732
  6.5 25.0 %copy-start.16 = (s32[3,4,12]{2,1,0:T(4,128)S(1)}, s32[3,4,12]{2,1,0:T(4,128)}, u32[]{:S(2)}) copy-start(s32[3,4,12]{2,1,0:T(4,128)} %param.11) | copy-start | bytes 1732
  6.5 25.1 %copy-start.23 = (s32[3,12]{1,0:T(4,128)S(1)}, s32[3,12]{1,0:T(4,128)}, u32[]{:S(2)}) copy-start(s32[3,12]{1,0:T(4,128)} %param.9) | copy-start | bytes 436
  6.5 85.5 %all-gather.2.cloned.1.call-start = ((), (), s32[]{:S(2)}) async-start(), calls=%async_computation | async-start | bytes 1966080 | tf_op jit(solution)/shard_map/all_gather | solution.py:52
  19.1 16.4 %collective-permute-start = (bf16[12,2,128,128]{3,2,1,0:T(8,128)(2,1)S(1)}, bf16[12,2,128,128]{3,2,1,0:T(8,128)(2,1)S(1)}, u32[]{:S(2)}, u32[]{:S(2)}) collective-permute-start(bf16[12,2,128,128]{3,2,1,0:T(8,128)(2,1)S(1)} %all_gather.6), channel_id=1, source_target_pairs={{0,4},{4,8},{8,12},{12,16},{16,20},{20,24},{24,28},{28,32},{32,36}... | collective-permute-start | bytes 2359304 | tf_op jit(solution)/shard_map/ppermute | solution.py:16
  26.6 13.6 %collective-permute-start.1 = (bf16[12,2,128,128]{3,2,1,0:T(8,128)(2,1)S(1)}, bf16[12,2,128,128]{3,2,1,0:T(8,128)(2,1)}, u32[]{:S(2)}, u32[]{:S(2)}) collective-permute-start(bf16[12,2,128,128]{3,2,1,0:T(8,128)(2,1)S(1)} %all_gather.6), channel_id=1, source_target_pairs={{4,0},{8,4},{12,8},{16,12},{20,16},{24,20},{28,24},{32,28},{36,32}... | collective-permute-start | bytes 2359304 | tf_op jit(solution)/shard_map/ppermute | solution.py:18
  35.5 0.9 copy-start.4
  44.8 1.4 copy-start.17
  47.0 1.4 copy-start.18
  49.2 1.3 copy-start.3
  49.2 1.3 copy-start.31
  49.2 1.3 copy-start.38
  50.5 2.0 %copy-start = (bf16[36,128,128]{1,2,0:T(8,128)(2,1)S(1)}, bf16[36,128,128]{1,2,0:T(8,128)(2,1)}, u32[]{:S(2)}) copy-start(bf16[36,128,128]{1,2,0:T(8,128)(2,1)} %copy.21) | copy-start | bytes 3538948
  50.5 2.0 %copy-start.13 = (bf16[3,12,128,128]{3,2,1,0:T(8,128)(2,1)S(1)}, bf16[3,12,128,128]{3,2,1,0:T(8,128)(2,1)}, u32[]{:S(2)}) copy-start(bf16[3,12,128,128]{3,2,1,0:T(8,128)(2,1)} %param.8) | copy-start | bytes 3538948
  50.5 2.0 %copy-start.30 = (pred[3,12]{1,0:T(4,128)(4,1)S(1)}, pred[3,12]{1,0:T(4,128)(4,1)}, u32[]{:S(2)}) copy-start(pred[3,12]{1,0:T(4,128)(4,1)} %get-tuple-element.49) | copy-start | bytes 112
  50.5 2.0 %copy-start.35 = (pred[3,12]{1,0:T(4,128)(4,1)S(1)}, pred[3,12]{1,0:T(4,128)(4,1)}, u32[]{:S(2)}) copy-start(pred[3,12]{1,0:T(4,128)(4,1)} %get-tuple-element.59) | copy-start | bytes 112
  52.5 2.6 %copy-start.5 = (f32[3,1,128,128]{2,3,0,1:T(8,128)}, f32[3,1,128,128]{2,3,0,1:T(8,128)S(1)}, u32[]{:S(2)}) copy-start(f32[3,1,128,128]{2,3,0,1:T(8,128)S(1)} %fusion.24) | copy-start | bytes 589828
  52.5 1.3 copy-start.1
  52.5 1.3 copy-start.29
  52.5 1.3 copy-start.36
  53.0 2.0 %copy-start.7 = (f32[3,1,128,128]{2,3,0,1:T(8,128)}, f32[3,1,128,128]{2,3,0,1:T(8,128)S(1)}, u32[]{:S(2)}) copy-start(f32[3,1,128,128]{2,3,0,1:T(8,128)S(1)} %fusion.25) | copy-start | bytes 589828
  53.8 0.7 copy-start.28
  53.8 0.7 copy-start.32
  54.3 0.7 copy-start.9
  55.1 0.7 copy-start.11
  55.7 42.1 %copy-start.22 = (s32[3,12]{1,0:T(4,128)S(1)}, s32[3,12]{1,0:T(4,128)}, u32[]{:S(2)}) copy-start(s32[3,12]{1,0:T(4,128)} %get-tuple-element.8) | copy-start | bytes 436
  55.7 42.2 %copy-start.21 = (s32[3,12]{1,0:T(4,128)S(1)}, s32[3,12]{1,0:T(4,128)}, u32[]{:S(2)}) copy-start(s32[3,12]{1,0:T(4,128)} %get-tuple-element.44) | copy-start | bytes 436
  55.7 42.3 %copy-start.20 = (s32[3,12]{1,0:T(4,128)S(1)}, s32[3,12]{1,0:T(4,128)}, u32[]{:S(2)}) copy-start(s32[3,12]{1,0:T(4,128)} %get-tuple-element.42) | copy-start | bytes 436
  55.7 42.3 %copy-start.19 = (s32[3,12]{1,0:T(4,128)S(1)}, s32[3,12]{1,0:T(4,128)}, u32[]{:S(2)}) copy-start(s32[3,12]{1,0:T(4,128)} %get-tuple-element.40) | copy-start | bytes 436
  92.1 21.5 %collective-permute-start.2 = (bf16[12,4,128,128]{2,3,0,1:T(8,128)(2,1)}, bf16[12,4,128,128]{2,3,0,1:T(8,128)(2,1)S(1)}, u32[]{:S(2)}, u32[]{:S(2)}) collective-permute-start(bf16[12,4,128,128]{2,3,0,1:T(8,128)(2,1)} %all-gather.2.cloned.1.call-done), channel_id=1, source_target_pairs={{0,4},{4,8},{8,12},{12,16},{16,20},{20,24},{24,28},{28,32},{32,36}... | collective-permute-start | bytes 4718600 | tf_op jit(solution)/shard_map/ppermute | solution.py:16
  95.9 22.2 %collective-permute-start.3 = (bf16[12,4,128,128]{2,3,0,1:T(8,128)(2,1)}, bf16[12,4,128,128]{2,3,0,1:T(8,128)(2,1)S(1)}, u32[]{:S(2)}, u32[]{:S(2)}) collective-permute-start(bf16[12,4,128,128]{2,3,0,1:T(8,128)(2,1)} %all-gather.2.cloned.1.call-done), channel_id=1, source_target_pairs={{4,0},{8,4},{12,8},{16,12},{20,16},{24,20},{28,24},{32,28},{36,32}... | collective-permute-start | bytes 4718600 | tf_op jit(solution)/shard_map/ppermute | solution.py:18
  144.4 0.8 copy-start.27
  144.4 0.8 copy-start.37
  145.1 2.3 %copy-start.14 = (bf16[3,12,128,128]{3,2,1,0:T(8,128)(2,1)S(1)}, bf16[3,12,128,128]{3,2,1,0:T(8,128)(2,1)}, u32[]{:S(2)}) copy-start(bf16[3,12,128,128]{3,2,1,0:T(8,128)(2,1)} %param.8) | copy-start | bytes 3538948
  145.2 2.3 %copy-start.26 = (pred[3,12]{1,0:T(4,128)(4,1)S(1)}, pred[3,12]{1,0:T(4,128)(4,1)}, u32[]{:S(2)}) copy-start(pred[3,12]{1,0:T(4,128)(4,1)} %get-tuple-element.43) | copy-start | bytes 112
  145.2 2.3 %copy-start.33 = (pred[3,12]{1,0:T(4,128)(4,1)S(1)}, pred[3,12]{1,0:T(4,128)(4,1)}, u32[]{:S(2)}) copy-start(pred[3,12]{1,0:T(4,128)(4,1)} %get-tuple-element.63) | copy-start | bytes 112
  147.4 1.3 copy-start.2
  147.5 1.3 copy-start.25
  147.5 1.3 copy-start.34
  148.7 0.6 copy-start.24
  149.3 0.9 copy-start.6
  149.3 1.0 copy-start.8
  149.3 1.1 copy-start.10
  149.3 1.2 copy-start.12
Sparse Core Ops, SparseCore 0:
  56.7 35.3 all-gather.1
where the time goes:
time: 159 us; the launch traced here: 158 us
  waiting for transfers between devices  58.7 us (37%)
  local copies, waits for them, and re-layouts  40.7 us (26%)
  starting transfers between devices  18.2 us (11%)
  between operations  14 us (9%)
  blocking collectives  11.6 us (7%)
  other arithmetic  8.08 us (5%)
  matrix products  7.26 us (5%)
    all_gather x1, waiting for transfers between devices, per_device(): domain_square = lax.all_gather(square_round, 'row', axis=0, tiled=True)  35.5 us
    gather x16, local copies, waits for them, and re-layouts, contract(): operand = jnp.take(flattened, position, axis=0)  24.8 us
    ppermute x2, waiting for transfers between devices, extended(): lax.ppermute(tail, axis, [(i, (i + 1) % count) for i in range(count)])  14.8 us
    all_gather x1, blocking collectives, per_device(): domain_window = lax.all_gather(window, 'row', axis=0, tiled=True)  11.6 us
    ppermute x2, starting transfers between devices, extended(): lax.ppermute(tail, axis, [(i, (i + 1) % count) for i in range(count)])  11.3 us
    ppermute x2, waiting for transfers between devices, extended(): lax.ppermute(head, axis, [((i + 1) % count, i) for i in range(count)])  8.38 us
    dot_general x8, matrix products, contract(): jnp.einsum('iaxy,iayz->ixz', p_blocks, operand, preferred_element_type=jn...  7.26 us
    ppermute x2, starting transfers between devices, extended(): lax.ppermute(head, axis, [((i + 1) % count, i) for i in range(count)])  6.89 us
  transfers between devices with their start and end apart: 5, of which 5 were waited for; matrix products, arithmetic and copies ran while one was open for 3% of the time, Pallas kernels for 0%

commit v1 on v0

v1 whole, which is shorter than its diff:
```python
import functools

import jax
import jax.numpy as jnp
from jax import lax
from jax.experimental import pallas as pl
from jax.experimental.pallas import tpu as pltpu
from jax.sharding import PartitionSpec as P

MW = 2
REACH = 2
SLOTS = 6
RIGHT, LEFT, OPPOSITE, ACROSS, SIDE = range(5)


class Spread:
    def __init__(self, buffer, unit, chunks, send_sem, recv_sem, place):
        self.buffer, self.unit, self.chunks = buffer, unit, chunks
        self.send_sem, self.recv_sem = send_sem, recv_sem
        self.x, self.right, self.left, self.across = place

    def rows(self, slot, k):
        offset, size, _ = self.chunks[k]
        return self.buffer.at[pl.ds(slot * self.unit + offset, size)]

    def copy(self, way, k):
        x = self.x
        opposite = 4 - 4 * (x // 2)
        if way == RIGHT:
            there = lax.rem(x + 1, 4)
            source, target, device = 2, 5 - 4 * ((there + 3) // 4), {"row": self.right}
        elif way == LEFT:
            there = lax.rem(x + 3, 4)
            source, target, device = 2, 3 + 2 * (there // 3), {"row": self.left}
        elif way == OPPOSITE:
            if self.chunks[k][2] == RIGHT:
                there = lax.rem(x + 1, 4)
                source, device = 5 - 4 * ((x + 3) // 4), {"row": self.right}
            else:
                there = lax.rem(x + 3, 4)
                source, device = 3 + 2 * (x // 3), {"row": self.left}
            target = 4 - 4 * (there // 2)
        elif way == ACROSS:
            source, target, device = opposite, 4 - opposite, {"dom": self.across}
        else:
            source, target, device = 5, 1 + 2 * (x // 3), {"dom": self.across}
        return pltpu.make_async_remote_copy(
            src_ref=self.rows(source, k),
            dst_ref=self.rows(target, k),
            send_sem=self.send_sem.at[way, k],
            recv_sem=self.recv_sem.at[way, k],
            device_id=device,
            device_id_type=pl.DeviceIdType.MESH,
        )

    def at_end(self, end, way, k, action):
        @pl.when(self.x == end)
        def _():
            getattr(self.copy(way, k), action)()

    def send(self, part):
        for way in (RIGHT, LEFT):
            for k in part:
                if self.chunks[k][2] == way:
                    self.copy(way, k).start()
        for way in (RIGHT, LEFT):
            for k in part:
                if self.chunks[k][2] != way:
                    self.copy(way, k).start()

    def arrive(self, way, k):
        self.copy(way, k).wait_recv()
        if way == RIGHT:
            self.at_end(0, SIDE, k, "start")
        else:
            self.at_end(3, SIDE, k, "start")

    def pass_on(self):
        every = range(len(self.chunks))
        for k in every:
            way = self.chunks[k][2]
            self.copy(way, k).wait_recv()
            self.copy(OPPOSITE, k).start()
            self.at_end(0 if way == RIGHT else 3, SIDE, k, "start")
        for k in every:
            way = LEFT if self.chunks[k][2] == RIGHT else RIGHT
            self.copy(way, k).wait_recv()
            self.at_end(0 if way == RIGHT else 3, SIDE, k, "start")
        for k in every:
            self.copy(OPPOSITE, k).wait_recv()
            self.copy(ACROSS, k).start()
        for k in every:
            self.at_end(0, SIDE, k, "wait_recv")
            self.at_end(3, SIDE, k, "wait_recv")
        for k in every:
            self.copy(ACROSS, k).wait_recv()

    def finish(self):
        for k in range(len(self.chunks)):
            for way in (RIGHT, LEFT, OPPOSITE, ACROSS):
                self.copy(way, k).wait_send()
            self.at_end(0, SIDE, k, "wait_send")
            self.at_end(3, SIDE, k, "wait_send")


def contract(blocks, nearby, zero, per_row, row, cols_ref, sel_ref, origin, clusters):
    count, products = cols_ref.shape[1], sel_ref.shape[1]
    total = None
    for pair in range(0, count, 2):
        left = jnp.concatenate([blocks[row, pair], blocks[row, pair + 1]], axis=1)
        right = []
        for a in (pair, pair + 1):
            base = lax.rem(cols_ref[row, a] - origin + clusters, clusters) * per_row
            line = []
            for s in range(products):
                picked = sel_ref[row, s, a]
                line.append(nearby[jnp.where(picked >= 0, jnp.minimum(base + picked, zero), zero)])
            right.append(jnp.concatenate(line, axis=1))
        term = jnp.dot(left, jnp.concatenate(right, axis=0), preferred_element_type=jnp.float32)
        total = term if total is None else total + term
    return total


def kernel(
    doms, p_hbm, cols_ref, sel_square_ref, sel_cube_ref, out_ref,
    blocks, window, square, total, local_sem, window_send, window_recv, square_send, square_recv,
):
    rows, products = out_ref.shape[0], out_ref.shape[1]
    size = out_ref.shape[2]
    x, dom = lax.axis_index("row"), lax.axis_index("dom")
    ahead, behind = lax.rem(dom + 1, doms), lax.rem(dom + doms - 1, doms)
    right, left = lax.rem(x + 1, 4), lax.rem(x + 3, 4)
    across = lax.rem(dom + doms + 1 - 2 * (x // 2), doms)
    clusters = doms * 4 * rows
    origin = ((dom * 4 + x) - REACH) * rows

    unit_w, unit_q = rows * MW, rows * products
    loads = [
        pltpu.make_async_copy(
            p_hbm.at[i, pl.ds(0, MW)], window.at[pl.ds(2 * unit_w + i * MW, MW)], local_sem.at[i]
        )
        for i in range(rows)
    ]
    loads.append(pltpu.make_async_copy(p_hbm, blocks, local_sem.at[rows]))
    for load in loads:
        load.start()

    barrier = pltpu.get_barrier_semaphore()
    for device in ({"row": right}, {"row": left}, {"dom": ahead}, {"dom": behind}):
        pl.semaphore_signal(barrier, inc=1, device_id=device, device_id_type=pl.DeviceIdType.MESH)
    zero_w, zero_q = SLOTS * unit_w, SLOTS * unit_q
    window[zero_w] = jnp.zeros((size, size), window.dtype)
    square[zero_q] = jnp.zeros((size, size), square.dtype)
    for load in loads[:rows]:
        load.wait()
    pl.semaphore_wait(barrier, 4)

    place = (x, right, left, across)
    half = unit_w // 2
    chunks = [(k, 1, RIGHT if k < half else LEFT) for k in range(unit_w)]
    first = Spread(window, unit_w, chunks, window_send, window_recv, place)
    pairs = products // 2
    chunks = [(k * pairs, pairs, RIGHT if k % 2 == 0 else LEFT) for k in range(2 * rows)]
    second = Spread(square, unit_q, chunks, square_send, square_recv, place)

    first.send(range(unit_w))
    first.pass_on()
    loads[rows].wait()
    for i in range(rows):
        value = contract(blocks, window, zero_w, MW, i, cols_ref, sel_square_ref, origin, clusters)
        total[i] = value
        for s in range(products):
            square[2 * unit_q + i * products + s] = value[:, s * size:(s + 1) * size].astype(square.dtype)
        second.send((2 * i, 2 * i + 1))
    second.pass_on()
    for i in range(rows):
        value = contract(blocks, square, zero_q, products, i, cols_ref, sel_cube_ref, origin, clusters)
        value = 3.0 * total[i] - 2.0 * value
        for s in range(products):
            out_ref[i, s] = value[:, s * size:(s + 1) * size].astype(out_ref.dtype)
    first.finish()
    second.finish()


def solution(mesh):
    doms, row_devices = mesh.shape["dom"], mesh.shape["row"]
    assert row_devices == 4

    def per_device(p_blocks, p_cols, sel_square, sel_cube):
        rows, count, size, _ = p_blocks.shape
        products = sel_square.shape[1]
        unit_w, unit_q = rows * MW, rows * products
        flops = 2 * 2 * rows * products * count * size**3
        return pl.pallas_call(
            functools.partial(kernel, doms),
            out_shape=jax.ShapeDtypeStruct((rows, products, size, size), jnp.bfloat16),
            in_specs=[pl.BlockSpec(memory_space=pl.ANY)] + [pl.BlockSpec(memory_space=pltpu.SMEM)] * 3,
            out_specs=pl.BlockSpec(memory_space=pltpu.VMEM),
            scratch_shapes=[
                pltpu.VMEM((rows, count, size, size), jnp.bfloat16),
                pltpu.VMEM((SLOTS * unit_w + 1, size, size), jnp.bfloat16),
                pltpu.VMEM((SLOTS * unit_q + 1, size, size), jnp.bfloat16),
                pltpu.VMEM((rows, size, products * size), jnp.float32),
                pltpu.SemaphoreType.DMA((rows + 1,)),
                pltpu.SemaphoreType.DMA((5, unit_w)),
                pltpu.SemaphoreType.DMA((5, unit_w)),
                pltpu.SemaphoreType.DMA((5, 2 * rows)),
                pltpu.SemaphoreType.DMA((5, 2 * rows)),
            ],
            cost_estimate=pl.CostEstimate(flops=flops, bytes_accessed=4 * p_blocks.size, transcendentals=0),
            compiler_params=pltpu.CompilerParams(
                collective_id=0, has_side_effects=True, vmem_limit_bytes=32 * 1024 * 1024
            ),
        )(p_blocks, p_cols, sel_square, sel_cube)

    return jax.shard_map(
        per_device,
        mesh=mesh,
        in_specs=(
            P(("dom", "row"), None, None, None),
            P(("dom", "row"), None),
            P(("dom", "row"), None, None),
            P(("dom", "row"), None, None),
        ),
        out_specs=P(("dom", "row"), None, None, None),
        check_vma=False,
    )
```

time: 159 us -> 50.1 us (0.32)
  the two profiles are of different devices: /device:TPU:1 before, /device:TPU:40 now
where the time goes in v1:
time: 50.1 us; the launch traced here: 49.9 us
  Pallas kernels  45.8 us (91%)
  local copies, waits for them, and re-layouts  4.08 us (8%)
    pallas_call x1, Pallas kernels, per_device(): pl.pallas_call(functools.partial(kernel, doms), out_shape=jax.ShapeDtypeS...  45.8 us
    unnamed x9, local copies, waits for them, and re-layouts  4.08 us

profile of v1, /device:TPU:40, one launch (start us, length us, event | category | flops | bytes accessed | tf_op | source)
XLA Modules:
  0.0 49.9 jit_solution(2154209519905526670)
XLA Ops:
  0.0 0.0 copy-start
  0.0 1.3 %copy-done = bf16[3,12,128,128]{3,2,1,0:T(8,128)(2,1)S(1)} copy-done((bf16[3,12,128,128]{3,2,1,0:T(8,128)(2,1)S(1)}, bf16[3,12,128,128]{3,2,1,0:T(8,128)(2,1)}, u32[]{:S(2)}) %copy-start) | copy-done | bytes 1179672
  1.3 0.0 copy-start.1
  1.3 0.7 %copy-done.1 = s32[3,4,12]{2,1,0:T(4,128)S(1)} copy-done((s32[3,4,12]{2,1,0:T(4,128)S(1)}, s32[3,4,12]{2,1,0:T(4,128)}, u32[]{:S(2)}) %copy-start.1) | copy-done | bytes 600
  2.0 0.0 copy-start.2
  2.0 0.7 %copy-done.2 = s32[3,4,12]{2,1,0:T(4,128)S(1)} copy-done((s32[3,4,12]{2,1,0:T(4,128)S(1)}, s32[3,4,12]{2,1,0:T(4,128)}, u32[]{:S(2)}) %copy-start.2) | copy-done | bytes 600
  2.7 0.0 copy-start.3
  2.7 0.7 %copy-done.3 = s32[3,12]{1,0:T(4,128)S(1)} copy-done((s32[3,12]{1,0:T(4,128)S(1)}, s32[3,12]{1,0:T(4,128)}, u32[]{:S(2)}) %copy-start.3) | copy-done | bytes 168
  3.3 45.8 %shard_map.46 = bf16[3,4,128,128]{3,2,1,0:T(8,128)(2,1)S(1)} custom-call(bf16[3,12,128,128]{3,2,1,0:T(8,128)(2,1)S(1)} %copy-done, s32[3,12]{1,0:T(4,128)S(1)} %copy-done.3, s32[3,4,12]{2,1,0:T(4,128)S(1)} %copy-done.1, s32[3,4,12]{2,1,0:T(4,128)S(1)} %copy-done.2), custom_call_target="tpu_custom_call" | custom-call | flops 1207959552 | bytes 2359296 | tf_op jit(solution)/shard_map/pallas_call | solution.py:194
  49.2 0.7 %copy.6 = bf16[3,4,128,128]{3,2,1,0:T(8,128)(2,1)} copy(bf16[3,4,128,128]{3,2,1,0:T(8,128)(2,1)S(1)} %shard_map.46) | data formatting | bytes 786432
Async XLA Ops:
  0.0 1.3 %copy-start = (bf16[3,12,128,128]{3,2,1,0:T(8,128)(2,1)S(1)}, bf16[3,12,128,128]{3,2,1,0:T(8,128)(2,1)}, u32[]{:S(2)}) copy-start(bf16[3,12,128,128]{3,2,1,0:T(8,128)(2,1)} %p_hbm.1) | copy-start | bytes 3538948
  1.3 0.7 %copy-start.1 = (s32[3,4,12]{2,1,0:T(4,128)S(1)}, s32[3,4,12]{2,1,0:T(4,128)}, u32[]{:S(2)}) copy-start(s32[3,4,12]{2,1,0:T(4,128)} %sel_square_ref.1) | copy-start | bytes 1732
  2.0 0.7 %copy-start.2 = (s32[3,4,12]{2,1,0:T(4,128)S(1)}, s32[3,4,12]{2,1,0:T(4,128)}, u32[]{:S(2)}) copy-start(s32[3,4,12]{2,1,0:T(4,128)} %sel_cube_ref.1) | copy-start | bytes 1732
  2.7 0.7 %copy-start.3 = (s32[3,12]{1,0:T(4,128)S(1)}, s32[3,12]{1,0:T(4,128)}, u32[]{:S(2)}) copy-start(s32[3,12]{1,0:T(4,128)} %cols_ref.1) | copy-start | bytes 436
